TPU v7x, 32 devices: a whole 2x2x4 slice. The times are simulated.
32 devices in a mesh: groups: 2 (over x), occ: 16 (over z, y, core).
Axes of the slice: x: 2, y: 2, z: 4, core: 2. Of those that a mesh axis runs over, the one named last changes fastest.
Arguments:
- factors: bfloat16 [32, 2, 512, 1024], P(('groups', 'occ')), parts along dimension 0, may hold values from -1.1953125 to 1.1953125
- occ_count: int32 [32], P('groups'), parts along dimension 0, may hold values from 1 to 2, as said below
- e_occ: float32 [32, 2], P('groups'), parts along dimension 0, may hold values from -2 to -0.3
- e_vir: float32 [1024], P('groups'), parts along dimension 0, may hold values from 0.5 to 3
- pair_flags: int32 [32, 2], P('groups'), parts along dimension 0, may hold values 0 or 1
Outputs:
- gamma_three: float32 [32, 2, 512, 1024], P(('groups', 'occ')), parts along dimension 0
- aux_density: float32 [2048, 1024], P(('groups', 'occ')), parts along dimension 0
There are 2 independent parts, one for each index of `groups`. A program takes and returns all parts, laid end to end along the dimension named above; each array names one. Nothing has to cross between parts.
Inputs may be any that keep to these rules, and one draw needn't show every extreme that they name: `occ_count`: some block has 2 live orbitals and some block has 1.
All inputs are finite; a program needn't handle non-finite values.
Results may differ from a plain program's by a relative error of at most 0.002.
Values may be sent and summed in bfloat16 or wider, within the bound.
A program may use at most 128 MiB of HBM per device.

v0:
```python
import functools

import jax
import jax.numpy as jnp
from jax import lax
from jax.experimental import pallas as pl
from jax.experimental.pallas import tpu as pltpu
from jax.sharding import PartitionSpec as P

MESH = pl.DeviceIdType.MESH
CHUNKS = 8


def kernel(
    n, occ_ref, e_occ_ref, flag_ref, own_hbm, vir_ref, gamma_hbm, aux_ref,
    own, slots, virt_sum, gamma, turned, prod, core_in, near_out, near_in, far_out, far_in,
    load_sem, save_sem, send_sem, recv_sem, core_send, core_recv, near_send, near_recv, far_send, far_recv,
):
    me = lax.axis_index("occ")
    core, near, far = me % 2, (me // 2) % 2, me // 4
    depth = n // 4
    orbitals, virtual, width = gamma.shape
    rows = own.shape[0] // CHUNKS
    part = width // n
    core_peer = me + 1 - 2 * core
    near_peer = me + 2 - 4 * near
    far_peer = (me + 4 - 8 * near + n) % n
    load = pltpu.make_async_copy(own_hbm, own, load_sem)
    load.start()

    def far_at(step):
        return (me + 4 * step) % n

    barrier = pltpu.get_barrier_semaphore()

    def greet(device):
        pl.semaphore_signal(barrier, inc=1, device_id={"occ": device}, device_id_type=MESH)

    greet(core_peer)
    greet(near_peer)

    @pl.loop(1, depth)
    def _(step):
        greet(far_at(step))

    row = jnp.broadcast_to(vir_ref[...], (virtual, virtual))
    virt_sum[...] = row + row.T
    load.wait()
    pl.semaphore_wait(barrier, depth + 1)

    def piece(source, slot, k, device):
        at = pl.ds(pl.multiple_of(k * rows, rows), rows)
        return pltpu.make_async_remote_copy(
            src_ref=source.at[at], dst_ref=slots.at[slot, at],
            send_sem=send_sem.at[slot, k], recv_sem=recv_sem.at[slot, k],
            device_id={"occ": device}, device_id_type=MESH,
        )

    @pl.loop(0, CHUNKS)
    def _(k):
        piece(own, 1, k, near_peer).start()
        piece(own, 0, k, core_peer).start()

    gamma[...] = jnp.zeros_like(gamma)
    relayed = 1 + (near + core) % 2
    per_orbital = CHUNKS // orbitals

    @pl.loop(0, 4 * orbitals)
    def _(t):
        late = t // (2 * orbitals)
        slot = (1 - late) * (t // orbitals) + late * (2 + t % 2)
        other = (1 - late) * (t % orbitals) + late * ((t - 2 * orbitals) // 2 % orbitals)

        @pl.loop(0, per_orbital)
        def _(j):
            k = other * per_orbital + j
            piece(own, slot, k, core_peer).wait_recv()

            @pl.when(slot == 1)
            def _():
                piece(slots.at[1], 2, k, far_peer).start()

            @pl.when(slot == relayed)
            def _():
                piece(slots.at[slot], 3, k, core_peer).start()

        wide = (slot + 1) // 2 % 2
        step = (1 - 2 * (slot // 2)) * ((1 - wide) * (1 - 2 * core) + wide * (2 - 4 * near))
        index = (me + step + n) % n
        first = (me + (1 - (step + 2) // 3) * (step + n)) % n
        live = flag_ref[first, wide].astype(jnp.float32) * jnp.where(other < occ_ref[index], 1.0, 0.0)
        right = slots[slot, pl.ds(pl.multiple_of(other * virtual, virtual), virtual)]
        for o in range(orbitals):
            scale = live * jnp.where(o < occ_ref[me], 1.0, 0.0)
            integrals = lax.dot_general(
                own[o * virtual:(o + 1) * virtual], right, (((1,), (1,)), ((), ())),
                preferred_element_type=jnp.float32,
            )
            denominator = virt_sum[...] - e_occ_ref[me, o] - e_occ_ref[index, other]
            weighted = (integrals.T - 2.0 * integrals) * (scale / denominator)
            gamma[o] += jnp.dot(weighted.astype(jnp.bfloat16), right, preferred_element_type=jnp.float32)

    save = pltpu.make_async_copy(gamma, gamma_hbm, save_sem)
    save.start()
    for o in range(orbitals):
        turned[:, o * virtual:(o + 1) * virtual] = gamma[o].T.astype(jnp.bfloat16)

    def core_copy(j):
        return pltpu.make_async_remote_copy(
            src_ref=prod.at[j, 1 - core], dst_ref=core_in.at[j],
            send_sem=core_send.at[j], recv_sem=core_recv.at[j],
            device_id={"occ": core_peer}, device_id_type=MESH,
        )

    def near_copy(j):
        return pltpu.make_async_remote_copy(
            src_ref=near_out.at[j], dst_ref=near_in.at[j],
            send_sem=near_send.at[j], recv_sem=near_recv.at[j],
            device_id={"occ": near_peer}, device_id_type=MESH,
        )

    def far_copy(j):
        return pltpu.make_async_remote_copy(
            src_ref=far_out.at[j], dst_ref=far_in.at[j],
            send_sem=far_send.at[j], recv_sem=far_recv.at[j],
            device_id={"occ": far_at(j + 1)}, device_id_type=MESH,
        )

    @pl.loop(0, depth)
    def _(j):
        target = (far + j + 1) % depth
        block = jnp.dot(
            turned[pl.ds(pl.multiple_of(target * 4 * part, 4 * part), 4 * part)], own[...],
            preferred_element_type=jnp.float32,
        )
        for c in range(2):
            for y in range(2):
                at = (2 * y + c) * part
                prod[j, c, y] = block[at:at + part]
        core_copy(j).start()

    @pl.loop(0, depth)
    def _(j):
        core_copy(j).wait_recv()
        near_out[j] = prod[j, core, 1 - near] + core_in[j, 1 - near]
        near_copy(j).start()
        far_out[j] = prod[j, core, near] + core_in[j, near]

    @pl.loop(0, depth - 1)
    def _(j):
        near_copy(j).wait_recv()
        far_out[j] += near_in[j]
        far_copy(j).start()

    near_copy(depth - 1).wait_recv()
    aux_ref[...] = far_out[depth - 1] + near_in[depth - 1]

    @pl.loop(0, depth - 1)
    def _(j):
        far_copy(j).wait_recv()
        aux_ref[...] += far_in[j]

    aux_ref[...] = aux_ref[...] * (1.0 / n)

    @pl.loop(0, CHUNKS)
    def _(k):
        piece(own, 0, k, core_peer).wait_send()
        piece(own, 1, k, near_peer).wait_send()
        piece(own, 2, k, far_peer).wait_send()
        piece(own, 3, k, core_peer).wait_send()

    @pl.loop(0, depth)
    def _(j):
        core_copy(j).wait_send()
        near_copy(j).wait_send()

    @pl.loop(0, depth - 1)
    def _(j):
        far_copy(j).wait_send()

    save.wait()


def per_device(factors, occ_count, e_occ, e_vir, pair_flags):
    n = lax.axis_size("occ")
    _, orbitals, virtual, width = factors.shape
    height = orbitals * virtual
    depth, part = n // 4, width // n
    smem = pl.BlockSpec(memory_space=pltpu.SMEM)
    vmem = pl.BlockSpec(memory_space=pltpu.VMEM)
    anywhere = pl.BlockSpec(memory_space=pl.ANY)
    dma = pltpu.SemaphoreType.DMA
    gamma, aux = pl.pallas_call(
        functools.partial(kernel, n),
        out_shape=(
            jax.ShapeDtypeStruct((orbitals, virtual, width), jnp.float32),
            jax.ShapeDtypeStruct((part, width), jnp.float32),
        ),
        in_specs=[smem, smem, smem, anywhere, vmem],
        out_specs=(anywhere, vmem),
        scratch_shapes=[
            pltpu.VMEM((height, width), jnp.bfloat16),
            pltpu.VMEM((4, height, width), jnp.bfloat16),
            pltpu.VMEM((virtual, virtual), jnp.float32),
            pltpu.VMEM((orbitals, virtual, width), jnp.float32),
            pltpu.VMEM((width, height), jnp.bfloat16),
            pltpu.VMEM((depth, 2, 2, part, width), jnp.float32),
            pltpu.VMEM((depth, 2, part, width), jnp.float32),
            pltpu.VMEM((depth, part, width), jnp.float32),
            pltpu.VMEM((depth, part, width), jnp.float32),
            pltpu.VMEM((depth, part, width), jnp.float32),
            pltpu.VMEM((depth, part, width), jnp.float32),
            dma, dma,
            dma((4, CHUNKS)), dma((4, CHUNKS)),
            dma((depth,)), dma((depth,)),
            dma((depth,)), dma((depth,)),
            dma((depth,)), dma((depth,)),
        ],
        compiler_params=pltpu.CompilerParams(
            collective_id=0, has_side_effects=True, vmem_limit_bytes=56 * 1024 * 1024
        ),
    )(occ_count, e_occ, pair_flags, factors.reshape(height, width), e_vir.reshape(1, virtual))
    return (gamma[None], aux)


def solution(mesh):
    placed = (
        P(("groups", "occ"), None, None, None),
        P("groups"),
        P("groups", None),
        P("groups"),
        P("groups", None),
    )
    return jax.shard_map(
        per_device,
        mesh=mesh,
        in_specs=placed,
        out_specs=(P(("groups", "occ"), None, None, None), P(("groups", "occ"), None)),
        check_vma=False,
    )
```

profile of v0, /device:TPU:9, one launch (start us, length us, event | category | flops | bytes accessed | tf_op | source)
XLA Modules:
  0.0 111.2 jit_solution(14316631427667107350)
XLA Ops:
  0.6 1.4 %copy.7.e_occ_ref = f32[16,2]{1,0:T(8,128)} copy(f32[16,2]{0,1:T(2,128)} %param.7) | data formatting | bytes 256 | tf_op args[2]
  2.0 1.4 %copy.8.flag_ref = s32[16,2]{1,0:T(8,128)} copy(s32[16,2]{0,1:T(2,128)} %param.9) | data formatting | bytes 256 | tf_op args[4]
  3.3 102.3 %shard_map.68 = (f32[2,512,1024]{2,1,0:T(8,128)}, f32[64,1024]{1,0:T(8,128)}) custom-call(s32[16]{0:T(128)} %occ_ref.1, f32[16,2]{1,0:T(8,128)} %copy.7.e_occ_ref, s32[16,2]{1,0:T(8,128)} %copy.8.flag_ref, bf16[1024,1024]{1,0:T(8,128)(2,1)} %bitcast.4, f32[1,512]{1,0:T(1,128)} %bitcast.5), custom_call_target="tpu_custom_call" | custom-call | tf_op jit(solution)/shard_map/pallas_call | solution.py:193
  105.7 0.0 copy-start
  105.7 4.8 %copy.11 = f32[1,2,512,1024]{3,2,1,0:T(8,128)} copy(f32[1,2,512,1024]{3,2,1,0:T(8,128)} %bitcast.3) | data formatting | bytes 8388608
  110.5 0.0 copy-done
  110.5 0.7 copy.12
Async XLA Ops:
  105.7 4.8 %copy-start = (f32[64,1024]{1,0:T(8,128)S(1)}, f32[64,1024]{1,0:T(8,128)}, u32[]{:S(2)}) copy-start(f32[64,1024]{1,0:T(8,128)} %get-tuple-element.9) | copy-start | bytes 786436
where the time goes:
time: 111 us
  Pallas kernels  102 us (92%)
  local copies, waits for them, and re-layouts  8.24 us (7%)
    pallas_call x1, Pallas kernels, per_device(): pl.pallas_call(functools.partial(kernel, n), out_shape=(jax.ShapeDtypeStr...  102 us
    unnamed x6, local copies, waits for them, and re-layouts  8.24 us

commit v1 on v0

--- a/solution.py
+++ b/solution.py
@@ -12,9 +12,10 @@
 
 
 def kernel(
-    n, occ_ref, e_occ_ref, flag_ref, own_hbm, vir_ref, gamma_hbm, aux_ref,
+    n, occ_hbm, e_occ_hbm, flag_hbm, own_hbm, vir_hbm, gamma_hbm, aux_ref,
+    occ_ref, e_occ_ref, flag_ref, vir_ref,
     own, slots, virt_sum, gamma, turned, prod, core_in, near_out, near_in, far_out, far_in,
-    load_sem, save_sem, send_sem, recv_sem, core_send, core_recv, near_send, near_recv, far_send, far_recv,
+    small_sem, load_sem, save_sem, send_sem, recv_sem, core_send, core_recv, near_send, near_recv, far_send, far_recv,
 ):
     me = lax.axis_index("occ")
     core, near, far = me % 2, (me // 2) % 2, me // 4
@@ -27,6 +28,10 @@
     far_peer = (me + 4 - 8 * near + n) % n
     load = pltpu.make_async_copy(own_hbm, own, load_sem)
     load.start()
+    pairs = ((occ_hbm, occ_ref), (e_occ_hbm, e_occ_ref), (flag_hbm, flag_ref), (vir_hbm, vir_ref))
+    small = [pltpu.make_async_copy(a, b, small_sem.at[i]) for i, (a, b) in enumerate(pairs)]
+    for copy in small:
+        copy.start()
 
     def far_at(step):
         return (me + 4 * step) % n
@@ -43,24 +48,29 @@
     def _(step):
         greet(far_at(step))
 
+    pl.semaphore_wait(barrier, depth + 1)
+
+    def piece(source, slot, k, device):
+        at = pl.ds(pl.multiple_of(k * rows, rows), rows)
+        return pltpu.make_async_remote_copy(
+            src_ref=source.at[at], dst_ref=slots.at[slot, at],
+            send_sem=send_sem.at[slot, k], recv_sem=recv_sem.at[slot, k],
+            device_id={"occ": device}, device_id_type=MESH,
+        )
+
+    @pl.loop(0, CHUNKS)
+    def _(k):
+        piece(own_hbm, 1, k, near_peer).start()
+
+    @pl.loop(0, CHUNKS)
+    def _(k):
+        piece(own_hbm, 0, k, core_peer).start()
+
+    for copy in small:
+        copy.wait()
     row = jnp.broadcast_to(vir_ref[...], (virtual, virtual))
     virt_sum[...] = row + row.T
     load.wait()
-    pl.semaphore_wait(barrier, depth + 1)
-
-    def piece(source, slot, k, device):
-        at = pl.ds(pl.multiple_of(k * rows, rows), rows)
-        return pltpu.make_async_remote_copy(
-            src_ref=source.at[at], dst_ref=slots.at[slot, at],
-            send_sem=send_sem.at[slot, k], recv_sem=recv_sem.at[slot, k],
-            device_id={"occ": device}, device_id_type=MESH,
-        )
-
-    @pl.loop(0, CHUNKS)
-    def _(k):
-        piece(own, 1, k, near_peer).start()
-        piece(own, 0, k, core_peer).start()
-
     gamma[...] = jnp.zeros_like(gamma)
     relayed = 1 + (near + core) % 2
     per_orbital = CHUNKS // orbitals
@@ -88,7 +98,7 @@
         step = (1 - 2 * (slot // 2)) * ((1 - wide) * (1 - 2 * core) + wide * (2 - 4 * near))
         index = (me + step + n) % n
         first = (me + (1 - (step + 2) // 3) * (step + n)) % n
-        live = flag_ref[first, wide].astype(jnp.float32) * jnp.where(other < occ_ref[index], 1.0, 0.0)
+        live = flag_ref[wide, first].astype(jnp.float32) * jnp.where(other < occ_ref[index], 1.0, 0.0)
         right = slots[slot, pl.ds(pl.multiple_of(other * virtual, virtual), virtual)]
         for o in range(orbitals):
             scale = live * jnp.where(o < occ_ref[me], 1.0, 0.0)
@@ -96,7 +106,7 @@
                 own[o * virtual:(o + 1) * virtual], right, (((1,), (1,)), ((), ())),
                 preferred_element_type=jnp.float32,
             )
-            denominator = virt_sum[...] - e_occ_ref[me, o] - e_occ_ref[index, other]
+            denominator = virt_sum[...] - e_occ_ref[o, me] - e_occ_ref[other, index]
             weighted = (integrals.T - 2.0 * integrals) * (scale / denominator)
             gamma[o] += jnp.dot(weighted.astype(jnp.bfloat16), right, preferred_element_type=jnp.float32)
 
@@ -105,6 +115,10 @@
     for o in range(orbitals):
         turned[:, o * virtual:(o + 1) * virtual] = gamma[o].T.astype(jnp.bfloat16)
 
+    def turn(j):
+        last = j // (depth - 1)
+        return (1 - last) * ((j + depth // 2 - 1) % (depth - 1) + 1)
+
     def core_copy(j):
         return pltpu.make_async_remote_copy(
             src_ref=prod.at[j, 1 - core], dst_ref=core_in.at[j],
@@ -123,12 +137,12 @@
         return pltpu.make_async_remote_copy(
             src_ref=far_out.at[j], dst_ref=far_in.at[j],
             send_sem=far_send.at[j], recv_sem=far_recv.at[j],
-            device_id={"occ": far_at(j + 1)}, device_id_type=MESH,
+            device_id={"occ": far_at(turn(j))}, device_id_type=MESH,
         )
 
     @pl.loop(0, depth)
     def _(j):
-        target = (far + j + 1) % depth
+        target = (far + turn(j)) % depth
         block = jnp.dot(
             turned[pl.ds(pl.multiple_of(target * 4 * part, 4 * part), 4 * part)], own[...],
             preferred_element_type=jnp.float32,
@@ -186,7 +200,6 @@
     _, orbitals, virtual, width = factors.shape
     height = orbitals * virtual
     depth, part = n // 4, width // n
-    smem = pl.BlockSpec(memory_space=pltpu.SMEM)
     vmem = pl.BlockSpec(memory_space=pltpu.VMEM)
     anywhere = pl.BlockSpec(memory_space=pl.ANY)
     dma = pltpu.SemaphoreType.DMA
@@ -196,9 +209,13 @@
             jax.ShapeDtypeStruct((orbitals, virtual, width), jnp.float32),
             jax.ShapeDtypeStruct((part, width), jnp.float32),
         ),
-        in_specs=[smem, smem, smem, anywhere, vmem],
+        in_specs=[pl.BlockSpec(memory_space=pltpu.HBM)] * 5,
         out_specs=(anywhere, vmem),
         scratch_shapes=[
+            pltpu.SMEM(occ_count.shape, jnp.int32),
+            pltpu.SMEM(e_occ.shape[::-1], jnp.float32),
+            pltpu.SMEM(pair_flags.shape[::-1], jnp.int32),
+            pltpu.VMEM((1, virtual), jnp.float32),
             pltpu.VMEM((height, width), jnp.bfloat16),
             pltpu.VMEM((4, height, width), jnp.bfloat16),
             pltpu.VMEM((virtual, virtual), jnp.float32),
@@ -210,7 +227,7 @@
             pltpu.VMEM((depth, part, width), jnp.float32),
             pltpu.VMEM((depth, part, width), jnp.float32),
             pltpu.VMEM((depth, part, width), jnp.float32),
-            dma, dma,
+            dma((4,)), dma, dma,
             dma((4, CHUNKS)), dma((4, CHUNKS)),
             dma((depth,)), dma((depth,)),
             dma((depth,)), dma((depth,)),
@@ -219,7 +236,7 @@
         compiler_params=pltpu.CompilerParams(
             collective_id=0, has_side_effects=True, vmem_limit_bytes=56 * 1024 * 1024
         ),
-    )(occ_count, e_occ, pair_flags, factors.reshape(height, width), e_vir.reshape(1, virtual))
+    )(occ_count, e_occ.T, pair_flags.T, factors.reshape(height, width), e_vir.reshape(1, virtual))
     return (gamma[None], aux)
 
 

time: 111 us -> 106 us (0.955)
  the two profiles are of different devices: /device:TPU:9 before, /device:TPU:6 now
where the time goes in v1:
time: 106 us
  Pallas kernels  99.5 us (94%)
  local copies, waits for them, and re-layouts  5.54 us (5%)
    pallas_call x1, Pallas kernels, per_device(): pl.pallas_call(functools.partial(kernel, n), out_shape=(jax.ShapeDtypeStr...  99.5 us
    unnamed x4, local copies, waits for them, and re-layouts  5.54 us

profile of v1, /device:TPU:6, one launch (start us, length us, event | category | flops | bytes accessed | tf_op | source)
XLA Modules:
  0.0 105.7 jit_solution(3062291417340371151)
XLA Ops:
  0.6 99.5 %shard_map.68 = (f32[2,512,1024]{2,1,0:T(8,128)}, f32[64,1024]{1,0:T(8,128)}) custom-call(s32[16]{0:T(128)} %occ_hbm.1, f32[2,16]{1,0:T(2,128)} %bitcast.8, s32[2,16]{1,0:T(2,128)} %bitcast.9, bf16[1024,1024]{1,0:T(8,128)(2,1)} %bitcast.6, f32[1,512]{1,0:T(1,128)} %bitcast.7), custom_call_target="tpu_custom_call" | custom-call | tf_op jit(solution)/shard_map/pallas_call | solution.py:206
  100.1 0.0 copy-start
  100.1 4.8 %copy.9 = f32[1,2,512,1024]{3,2,1,0:T(8,128)} copy(f32[1,2,512,1024]{3,2,1,0:T(8,128)} %bitcast.5) | data formatting | bytes 8388608
  105.0 0.0 copy-done
  105.0 0.7 copy.10
Async XLA Ops:
  100.1 4.8 %copy-start = (f32[64,1024]{1,0:T(8,128)S(1)}, f32[64,1024]{1,0:T(8,128)}, u32[]{:S(2)}) copy-start(f32[64,1024]{1,0:T(8,128)} %get-tuple-element.9) | copy-start | bytes 786436

commit v2 on v1

--- a/solution.py
+++ b/solution.py
@@ -113,7 +113,7 @@
     save = pltpu.make_async_copy(gamma, gamma_hbm, save_sem)
     save.start()
     for o in range(orbitals):
-        turned[:, o * virtual:(o + 1) * virtual] = gamma[o].T.astype(jnp.bfloat16)
+        turned[:, o * virtual:(o + 1) * virtual] = gamma[o].astype(jnp.bfloat16).T
 
     def turn(j):
         last = j // (depth - 1)
@@ -140,25 +140,28 @@
             device_id={"occ": far_at(turn(j))}, device_id_type=MESH,
         )
 
-    @pl.loop(0, depth)
-    def _(j):
-        target = (far + turn(j)) % depth
-        block = jnp.dot(
-            turned[pl.ds(pl.multiple_of(target * 4 * part, 4 * part), 4 * part)], own[...],
-            preferred_element_type=jnp.float32,
-        )
-        for c in range(2):
-            for y in range(2):
-                at = (2 * y + c) * part
-                prod[j, c, y] = block[at:at + part]
-        core_copy(j).start()
-
-    @pl.loop(0, depth)
-    def _(j):
-        core_copy(j).wait_recv()
-        near_out[j] = prod[j, core, 1 - near] + core_in[j, 1 - near]
-        near_copy(j).start()
-        far_out[j] = prod[j, core, near] + core_in[j, near]
+    @pl.loop(0, depth + 1)
+    def _(j):
+        @pl.when(j < depth)
+        def _():
+            target = (far + turn(j)) % depth
+            block = jnp.dot(
+                turned[pl.ds(pl.multiple_of(target * 4 * part, 4 * part), 4 * part)], own[...],
+                preferred_element_type=jnp.float32,
+            )
+            for c in range(2):
+                for y in range(2):
+                    at = (2 * y + c) * part
+                    prod[j, c, y] = block[at:at + part]
+            core_copy(j).start()
+
+        @pl.when(j > 0)
+        def _():
+            i = j - 1
+            core_copy(i).wait_recv()
+            near_out[i] = prod[i, core, 1 - near] + core_in[i, 1 - near]
+            near_copy(i).start()
+            far_out[i] = prod[i, core, near] + core_in[i, near]
 
     @pl.loop(0, depth - 1)
     def _(j):

time: 106 us -> 106 us (level)
  the two profiles are of different devices: /device:TPU:6 before, /device:TPU:9 now
where the time goes in v2:
time: 106 us
  Pallas kernels  99.8 us (94%)
  local copies, waits for them, and re-layouts  5.54 us (5%)
    pallas_call x1, Pallas kernels, per_device(): pl.pallas_call(functools.partial(kernel, n), out_shape=(jax.ShapeDtypeStr...  99.8 us
    unnamed x4, local copies, waits for them, and re-layouts  5.54 us

profile of v2, /device:TPU:9, one launch (start us, length us, event | category | flops | bytes accessed | tf_op | source)
XLA Modules:
  0.0 106.0 jit_solution(8898540452502392855)
XLA Ops:
  0.6 99.8 %shard_map.68 = (f32[2,512,1024]{2,1,0:T(8,128)}, f32[64,1024]{1,0:T(8,128)}) custom-call(s32[16]{0:T(128)} %occ_hbm.1, f32[2,16]{1,0:T(2,128)} %bitcast.8, s32[2,16]{1,0:T(2,128)} %bitcast.9, bf16[1024,1024]{1,0:T(8,128)(2,1)} %bitcast.6, f32[1,512]{1,0:T(1,128)} %bitcast.7), custom_call_target="tpu_custom_call" | custom-call | tf_op jit(solution)/shard_map/pallas_call | solution.py:209
  100.4 0.0 copy-start
  100.4 4.8 %copy.9 = f32[1,2,512,1024]{3,2,1,0:T(8,128)} copy(f32[1,2,512,1024]{3,2,1,0:T(8,128)} %bitcast.5) | data formatting | bytes 8388608
  105.3 0.0 copy-done
  105.3 0.7 copy.10
Async XLA Ops:
  100.4 4.8 %copy-start = (f32[64,1024]{1,0:T(8,128)S(1)}, f32[64,1024]{1,0:T(8,128)}, u32[]{:S(2)}) copy-start(f32[64,1024]{1,0:T(8,128)} %get-tuple-element.9) | copy-start | bytes 786436
